TPU v7x, 512 devices: a whole 4x4x16 slice. The times are simulated.
512 devices in a mesh: ctx: 128 (over x, z, core), ch: 4 (over y).
Axes of the slice: x: 4, y: 4, z: 16, core: 2. Of those that a mesh axis runs over, the one named last changes fastest.
Arguments:
- inputs_x: bfloat16 [16384, 2048], P('ctx', 'ch'), may hold values from -6 to 6
- grad_out: bfloat16 [16384, 2048], P('ctx', 'ch'), may hold values from -0.0625 to 0.0625
- filter_blocks: float32 [128, 128, 512], P('ctx'), may hold values from -12 to 12
- lag_block: int32 [128], replicated, may hold values from 0 to 127, each once
Outputs:
- grad_inputs: bfloat16 [16384, 2048], P('ctx', 'ch')
- grad_filter: float32 [128, 128, 512], P('ctx', None, 'ch')
Inputs may be any that keep to these rules, and one draw needn't show every extreme that they name: Each value appears once: row q of filter_blocks holds lags lag_block[q] * 128 to lag_block[q] * 128 + 127.
All inputs are finite; a program needn't handle non-finite values.
Results may differ from a plain program's by a relative error of at most 0.001.
Values sent between devices are 32-bit elements; how exact they have to be, the bound alone decides.
A program may use at most 128 MiB of HBM per device.

v0:
```python
import math

import jax
import jax.numpy as jnp
from jax import lax
from jax.sharding import PartitionSpec as P


def exact_dot(left, right):
    return jnp.dot(left, right, precision=lax.Precision.HIGHEST, preferred_element_type=jnp.float32)


def phase_angle(left_idx, right_idx, period):
    product = left_idx[:, None] * right_idx[None, :] % period
    return 2.0 * math.pi / period * product.astype(jnp.float32)


def block_forward(block_rows):
    freqs = jnp.arange(block_rows, dtype=jnp.int32)
    angle = phase_angle(freqs, freqs, 2 * block_rows)
    parity = (1 - 2 * (freqs % 2)).astype(jnp.float32)
    sine_rows = jnp.where(freqs[:, None] == 0, parity[None, :], -jnp.sin(angle))
    return jnp.concatenate([jnp.cos(angle), sine_rows], axis=0)


def block_inverse(block_rows):
    freqs = jnp.arange(block_rows, dtype=jnp.int32)
    angle = phase_angle(freqs, freqs, 2 * block_rows)
    factor = 1.0 / (2 * block_rows)
    parity = (1 - 2 * (freqs % 2)).astype(jnp.float32)
    weight = jnp.where(freqs == 0, 1.0, 2.0) * factor
    cosine_cols = jnp.cos(angle) * weight[None, :]
    sine_cols = jnp.where(
        freqs[None, :] == 0, parity[:, None] * factor, -2.0 * factor * jnp.sin(angle)
    )
    return jnp.concatenate([cosine_cols, sine_cols], axis=1)


def conj_product(a_real, a_imag, b_real, b_imag):
    return (a_real * b_real + a_imag * b_imag, a_imag * b_real - a_real * b_imag)


def correlate(left_hat, right_hat, packed):
    left_real, left_imag = left_hat
    right_real, right_imag = right_hat
    prod_00 = conj_product(left_real[:, 0], left_imag[:, 0], right_real[:, 0], right_imag[:, 0])
    prod_11 = conj_product(left_real[:, 1], left_imag[:, 1], right_real[:, 1], right_imag[:, 1])
    prod_01 = conj_product(left_real[:, 0], left_imag[:, 0], right_real[:, 1], right_imag[:, 1])
    prod_10 = conj_product(left_real[:, 1], left_imag[:, 1], right_real[:, 0], right_imag[:, 0])
    spread = 1.0 - packed
    first = [prod_00[part] - spread * prod_11[part] for part in range(2)]
    second = [
        spread * (prod_01[part] + prod_10[part]) + packed * prod_11[part] for part in range(2)
    ]
    return (jnp.stack([first[0], second[0]], axis=1), jnp.stack([first[1], second[1]], axis=1))


def body(inputs_x, grad_out, filter_blocks, lag_block):
    block_rows, width = inputs_x.shape
    ctx_count = lax.axis_size("ctx")
    band_bins = block_rows // ctx_count
    fwd_table = block_forward(block_rows)
    joined = jnp.concatenate(
        [grad_out.astype(jnp.float32), inputs_x.astype(jnp.float32), filter_blocks[0]], axis=1
    )
    spectra = exact_dot(fwd_table, joined).reshape(1, 2, block_rows, 3, width)
    bands = lax.all_to_all(spectra, "ctx", split_axis=2, concat_axis=0, tiled=True)
    bin_index = lax.axis_index("ctx") * band_bins + jnp.arange(band_bins, dtype=jnp.int32)
    packed = (bin_index == 0).astype(jnp.float32)[:, None]
    parity = (1 - 2 * (bin_index % 2)).astype(jnp.float32)[:, None]
    band_cot = bands[:, :, :, 0]
    band_act = bands[:, :, :, 1]
    band_filt = bands[:, :, :, 2][jnp.argsort(lag_block)]
    window = band_filt + parity * jnp.concatenate(
        [jnp.zeros_like(band_filt[:1]), band_filt[:-1]], axis=0
    )
    flip = jnp.stack([jnp.ones_like(packed), 2.0 * packed - 1.0])
    stacked = jnp.stack([band_cot, band_act * flip, window * flip], axis=1)
    outer_len = 2 * ctx_count
    angle = phase_angle(
        jnp.arange(outer_len, dtype=jnp.int32), jnp.arange(ctx_count, dtype=jnp.int32), outer_len
    )
    outer_cos = jnp.cos(angle)
    outer_sin = jnp.sin(angle)
    flat = stacked.reshape(ctx_count, -1)
    hat_real = exact_dot(outer_cos, flat).reshape(outer_len, 3, 2, band_bins, width)
    hat_imag = (-exact_dot(outer_sin, flat)).reshape(outer_len, 3, 2, band_bins, width)
    cot_hat = (hat_real[:, 0], hat_imag[:, 0])
    act_hat = (hat_real[:, 1], hat_imag[:, 1])
    win_hat = (hat_real[:, 2], hat_imag[:, 2])
    lag_real, lag_imag = correlate(cot_hat, act_hat, packed)
    inp_real, inp_imag = correlate(cot_hat, win_hat, packed)
    real_flat = jnp.stack([lag_real, inp_real], axis=1).reshape(outer_len, -1)
    imag_flat = jnp.stack([lag_imag, inp_imag], axis=1).reshape(outer_len, -1)
    inverted = (exact_dot(outer_cos.T, real_flat) - exact_dot(outer_sin.T, imag_flat)) / outer_len
    inverted = inverted.reshape(ctx_count, 2, 2, band_bins, width)
    lag_spec = inverted[:, 0]
    grad_spec = inverted[:, 1]
    shifted = jnp.concatenate([lag_spec[1:], jnp.zeros_like(lag_spec[:1])], axis=0)
    lag_total = lag_spec + parity * shifted
    lag_mine = lag_total[lag_block]
    inv_table = block_inverse(block_rows)
    returned = lax.all_to_all(
        jnp.stack([grad_spec, lag_mine], axis=1), "ctx", split_axis=0, concat_axis=3, tiled=True
    )
    grad_rows = returned[0, 0].reshape(2 * block_rows, width)
    lag_rows = returned[0, 1].reshape(2 * block_rows, width)
    grad_inputs = exact_dot(inv_table, grad_rows).astype(jnp.bfloat16)
    grad_filter = lax.psum_scatter(
        exact_dot(inv_table, lag_rows), "ch", scatter_dimension=1, tiled=True
    )
    return (grad_inputs, grad_filter[None])


def solution(mesh):
    in_specs = (P("ctx", "ch"), P("ctx", "ch"), P("ctx", None, None), P())
    out_specs = (P("ctx", "ch"), P("ctx", None, "ch"))
    return jax.shard_map(body, mesh=mesh, in_specs=in_specs, out_specs=out_specs, check_vma=False)
```

profile of v0, /device:TPU:1, one launch (start us, length us, event | category | flops | bytes accessed | tf_op | source)
XLA Modules:
  0.0 259.0 jit_solution(7318269752613340707)
XLA Ops:
  7.2 0.9 convert_element_type.52
  8.1 0.9 convert_element_type.51
  9.1 0.3 multiply_select_fusion
  9.4 2.4 fusion.3
  11.7 0.8 reshape.322
  12.6 2.2 copy.44
  14.8 20.5 %all-to-all-start = ((f32[1,2,128,3,512]{4,1,3,0,2:T(2,128)}), f32[1,2,128,3,512]{4,1,3,0,2:T(2,128)S(1)}, u32[]{:S(2)}, u32[]{:S(2)}) async-start(f32[1,2,128,3,512]{4,1,3,0,2:T(2,128)} %copy.44), calls=%async_computation | async-start | bytes 3145728 | tf_op jit(solution)/shard_map/all_to_all | solution.py:67
  35.3 0.0 copy-done.10
  35.4 2.5 sort.17
  37.9 0.1 maximum_bitcast_fusion.4
  38.0 74.1 %all-to-all-done = f32[1,2,128,3,512]{4,1,3,0,2:T(2,128)S(1)} async-done(((f32[1,2,128,3,512]{4,1,3,0,2:T(2,128)}), f32[1,2,128,3,512]{4,1,3,0,2:T(2,128)S(1)}, u32[]{:S(2)}, u32[]{:S(2)}) %all-to-all-start) | async-done | bytes 1572896 | tf_op jit(solution)/shard_map/all_to_all | solution.py:67
  112.1 0.5 copy.70
  112.6 0.4 slice_bitcast_fusion.7
  113.0 0.2 fusion.11
  113.2 1.1 gather_fusion
  114.4 0.3 fusion.13
  114.8 0.7 pad_maximum_fusion.2
  115.5 0.7 copy.46
  116.2 0.0 copy-start
  116.2 3.1 %fusion.1 = f32[256,3,2,512]{3,0,2,1:T(8,128)S(1)} fusion(f32[128,3,2,1,512]{0,4,2,1,3:T(8,128)S(1)} %copy.46), kind=kOutput, calls=%fused_computation.8 | convolution fusion | flops 1208418304 | bytes 4718592 | tf_op jit(solution)/shard_map/dot_general | solution.py:10
  119.4 0.0 copy-done
  119.4 0.1 slice_bitcast_fusion
  119.5 1.2 slice_bitcast_fusion.1
  120.7 0.6 copy-done.1
  121.3 4.8 %convolution_negate_fusion = f32[256,3072]{1,0:T(8,128)} fusion(f32[128,3072]{0,1:T(8,128)S(1)} %bitcast.107), kind=kOutput, calls=%fused_computation.2 | convolution fusion | flops 1209204736 | bytes 4718592 | tf_op jit(solution)/shard_map/dot_general | solution.py:10
  126.1 3.5 %copy.49 = f32[256,3072]{0,1:T(8,128)} copy(f32[256,3072]{1,0:T(8,128)} %convolution_negate_fusion) | data formatting | bytes 6291456 | tf_op jit(solution)/shard_map/neg | solution.py:87
  129.6 3.6 %fusion.62 = (f32[256,1,2,1,512]{0,4,2,1,3:T(8,128)}, f32[256,1,2,1,512]{0,4,2,1,3:T(8,128)}, f32[256,1,2,1,512]{0,4,2,1,3:T(8,128)}) fusion(f32[256,3,2,1,512]{0,4,2,1,3:T(8,128)} %bitcast.108), kind=kLoop, calls=%fused_computation.115 | loop fusion | bytes 6291456 | tf_op jit(solution)/shard_map/slice | solution.py:89
  133.2 1.6 copy.62
  134.8 2.6 copy.64
  137.4 2.8 %multiply_subtract_fusion.4 = (f32[256,1,1,512]{3,0,1,2:T(8,128)}, f32[256,1,1,512]{3,0,1,2:T(8,128)}) fusion(f32[256,2,1,512]{3,0,1,2:T(8,128)} %bitcast.113, f32[256,2,1,512]{3,0,1,2:T(8,128)S(1)} %slice_bitcast_fusion, f32[256,2,1,512]{3,0,1,2:T(8,128)S(1)} %bitcast.103, f32[256,2,1,512]{3,0,1,2:T(8,128)S(1)} %get-tuple-element.13, f32[]{:T(128)} %bitcast.29, ...), kind=kLoop, calls=%fused_computation.45 | loop fusion | flops 2359296 | bytes 5242888 | tf_op jit(solution)/shard_map/sub | solution.py:51
  140.1 1.5 multiply_subtract_fusion
  141.6 1.6 copy.63
  143.2 2.8 %multiply_subtract_fusion.5 = (f32[256,1,1,512]{3,0,1,2:T(8,128)}, f32[256,1,1,512]{3,0,1,2:T(8,128)}) fusion(f32[256,2,1,512]{3,0,1,2:T(8,128)S(1)} %bitcast.111, f32[256,2,1,512]{3,0,1,2:T(8,128)} %get-tuple-element.12, f32[256,2,1,512]{3,0,1,2:T(8,128)S(1)} %bitcast.105, f32[256,2,1,512]{3,0,1,2:T(8,128)S(1)} %get-tuple-element.13, f32[]{:T(128)} %bitcast.29, ...), kind=kLoop, calls=%fused_computation.48 | loop fusion | flops 2359296 | bytes 5242888 | tf_op jit(solution)/shard_map/sub | solution.py:51
  146.0 0.0 copy-done.3
  146.0 0.5 multiply_subtract_fusion.2
  146.6 0.5 copy-done.8
  147.1 0.2 copy-done.9
  147.2 0.1 maximum_bitcast_fusion.3
  147.3 0.1 maximum_bitcast_fusion.2
  147.4 1.5 pad_maximum_fusion.1
  148.9 2.0 copy.54
  150.9 0.1 maximum_bitcast_fusion.1
  151.0 0.9 copy-done.6
  151.9 0.2 copy-done.7
  152.1 0.1 maximum_bitcast_fusion
  152.2 1.5 pad_maximum_fusion
  153.7 2.9 %copy.53 = f32[256,2,2,1,512]{0,4,2,1,3:T(8,128)} copy(f32[256,2,2,1,512]{4,0,2,3,1:T(8,128)} %pad_maximum_fusion) | data formatting | bytes 4194304 | tf_op jit(solution)/shard_map/stack | solution.py:93
  156.6 4.4 %fusion.30 = f32[128,2048]{1,0:T(8,128)S(1)} fusion(f32[256,2048]{0,1:T(8,128)} %bitcast.116), kind=kOutput, calls=%fused_computation.76 | convolution fusion | flops 805765120 | bytes 3145728 | tf_op jit(solution)/shard_map/dot_general | solution.py:10
  161.0 2.8 %fusion = f32[128,2048]{1,0:T(8,128)S(1)} fusion(f32[128,2048]{1,0:T(8,128)S(1)} %fusion.30, f32[256,2048]{0,1:T(8,128)S(1)} %bitcast.115), kind=kOutput, calls=%fused_computation.4 | convolution fusion | flops 806289408 | bytes 4194304 | tf_op jit(solution)/shard_map/dot_general | solution.py:10
  163.8 0.9 reshape.328
  164.8 0.3 fusion.10
  165.0 1.1 gather_fusion.1
  166.2 0.5 pad_maximum_fusion.3
  166.6 1.3 copy.58
  168.0 8.6 %all-to-all-start.1 = ((f32[128,2,2,1,512]{4,2,3,1,0:T(2,128)}), f32[128,2,2,1,512]{4,2,3,1,0:T(2,128)S(1)}, u32[]{:S(2)}, u32[]{:S(2)}) async-start(f32[128,2,2,1,512]{4,2,3,1,0:T(2,128)} %copy.58), calls=%async_computation.1 | async-start | bytes 2097152 | tf_op jit(solution)/shard_map/all_to_all | solution.py:103
  176.6 0.0 reduce-scatter.2.cloned.1.call-start
  176.6 0.3 broadcast_multiply_fusion
  176.9 54.0 %all-to-all-done.1 = f32[128,2,2,1,512]{4,2,3,1,0:T(2,128)S(1)} async-done(((f32[128,2,2,1,512]{4,2,3,1,0:T(2,128)}), f32[128,2,2,1,512]{4,2,3,1,0:T(2,128)S(1)}, u32[]{:S(2)}, u32[]{:S(2)}) %all-to-all-start.1) | async-done | bytes 1048608 | tf_op jit(solution)/shard_map/all_to_all | solution.py:103
  230.9 0.3 copy.71
  231.3 0.1 fusion.63
  231.4 1.1 fusion.24
  232.5 0.0 reduce-scatter.2.cloned.1.call-update
  232.5 1.1 convolution_convert_fusion
  233.6 18.5 %reduce-scatter.2.cloned.1.call-done = f32[128,128]{1,0:T(8,128)} async-done(((f32[128,512]{1,0:T(8,128)}), f32[128,128]{1,0:T(8,128)}) %reduce-scatter.2.cloned.1.call-update) | async-done | bytes 65552 | tf_op jit(solution)/shard_map/reduce_scatter | solution.py:109
  (25 shorter events, 0.2 us)
Async XLA Ops:
  14.8 20.6 %copy-start.10 = (s32[128]{0:T(128)S(1)}, s32[128]{0:T(128)}, u32[]{:S(2)}) copy-start(s32[128]{0:T(128)} %param.7) | copy-start | bytes 1540
  14.8 97.3 %all-to-all-start = ((f32[1,2,128,3,512]{4,1,3,0,2:T(2,128)}), f32[1,2,128,3,512]{4,1,3,0,2:T(2,128)S(1)}, u32[]{:S(2)}, u32[]{:S(2)}) async-start(f32[1,2,128,3,512]{4,1,3,0,2:T(2,128)} %copy.44), calls=%async_computation | async-start | bytes 3145728 | tf_op jit(solution)/shard_map/all_to_all | solution.py:67
  116.2 3.2 %copy-start = (f32[128,3,2,1,512]{0,4,2,1,3:T(8,128)}, f32[128,3,2,1,512]{0,4,2,1,3:T(8,128)S(1)}, u32[]{:S(2)}) copy-start(f32[128,3,2,1,512]{0,4,2,1,3:T(8,128)S(1)} %copy.46) | copy-start | bytes 4718596
  119.5 1.8 copy-start.1
  137.4 2.8 %copy-start.2 = (f32[256,1,2,1,512]{4,0,2,3,1:T(8,128)S(1)}, f32[256,1,2,1,512]{4,0,2,3,1:T(8,128)}, u32[]{:S(2)}) copy-start(f32[256,1,2,1,512]{4,0,2,3,1:T(8,128)} %copy.64) | copy-start | bytes 3145732
  143.2 2.8 %copy-start.3 = (f32[256,2,1,512]{3,0,1,2:T(8,128)S(1)}, f32[256,2,1,512]{3,0,1,2:T(8,128)}, u32[]{:S(2)}) copy-start(f32[256,2,1,512]{3,0,1,2:T(8,128)} %get-tuple-element.12) | copy-start | bytes 3145732
  146.0 1.0 copy-start.8
  146.0 1.2 copy-start.9
  148.9 2.0 copy-start.4
  148.9 2.0 copy-start.5
  150.9 1.0 copy-start.6
  150.9 1.2 copy-start.7
  168.0 62.9 %all-to-all-start.1 = ((f32[128,2,2,1,512]{4,2,3,1,0:T(2,128)}), f32[128,2,2,1,512]{4,2,3,1,0:T(2,128)S(1)}, u32[]{:S(2)}, u32[]{:S(2)}) async-start(f32[128,2,2,1,512]{4,2,3,1,0:T(2,128)} %copy.58), calls=%async_computation.1 | async-start | bytes 2097152 | tf_op jit(solution)/shard_map/all_to_all | solution.py:103
  176.6 75.5 %reduce-scatter.2.cloned.1.call-start = ((), (), s32[]{:S(2)}) async-start(), calls=%async_computation.3 | async-start | bytes 327680 | tf_op jit(solution)/shard_map/reduce_scatter | solution.py:109
Sparse Core Ops, SparseCore 0:
  232.6 19.4 reduce-scatter.1
where the time goes:
time: 261 us; the launch traced here: 259 us
  waiting for transfers between devices  147 us (56%)
  local copies, waits for them, and re-layouts  31.1 us (12%)
  starting transfers between devices  29.2 us (11%)
  matrix products  19.7 us (8%)
  other arithmetic  17.9 us (7%)
  between operations  14.4 us (6%)
    all_to_all x1, waiting for transfers between devices, body(): lax.all_to_all(spectra, 'ctx', split_axis=2, concat_axis=0, tiled=True)  74.1 us
    all_to_all x1, waiting for transfers between devices, body(): lax.all_to_all(jnp.stack([grad_spec, lag_mine], axis=1), 'ctx', split_axi...  54 us
    all_to_all x1, starting transfers between devices, body(): lax.all_to_all(spectra, 'ctx', split_axis=2, concat_axis=0, tiled=True)  20.5 us
    dot_general x7, matrix products, exact_dot(): jnp.dot(left, right, precision=lax.Precision.HIGHEST, preferred_element_t...  19.7 us
    reduce_scatter x1, waiting for transfers between devices, body(): lax.psum_scatter(exact_dot(inv_table, lag_rows), 'ch', scatter_dimension=...  18.5 us
    all_to_all x1, starting transfers between devices, body(): lax.all_to_all(jnp.stack([grad_spec, lag_mine], axis=1), 'ctx', split_axi...  8.58 us
    unnamed x26, local copies, waits for them, and re-layouts  8.07 us
    sub x4, other arithmetic, correlate(): first = [prod_00[part] - spread * prod_11[part] for part in range(2)]  7.6 us
  transfers between devices with their start and end apart: 3, of which 3 were waited for; matrix products, arithmetic and copies ran while one was open for 2% of the time, Pallas kernels for 0%

commit v1 on v0

v1 whole, which is shorter than its diff:
```python
import jax
import jax.numpy as jnp
from jax import lax
from jax.experimental import pallas as pl
from jax.experimental.pallas import tpu as pltpu
from jax.sharding import PartitionSpec as P

BF = jnp.bfloat16
F32 = jnp.float32

def conv_kernel(d_ref, x_ref, h_ref, lagcol_ref, lagrow_ref, g_ref, l_ref, dpad, xpad, hpad, hbank, xbank, w_ref, gacc, lacc):
    col = lax.broadcasted_iota(jnp.int32, (128, 128), 1)
    row = lax.broadcasted_iota(jnp.int32, (128, 128), 0)
    flip = (row + col == 127).astype(BF)
    take = (lagrow_ref[...] == row).astype(F32)
    h = jnp.dot(take, h_ref[...], precision=lax.Precision.HIGHEST, preferred_element_type=F32)
    hi = h.astype(BF)
    lo = (h - hi.astype(F32)).astype(BF)
    zeros = jnp.zeros((16, 128), F32)
    for part, val in enumerate((hi, lo)):
        hpad[part, pl.ds(0, 16), :] = zeros
        hpad[part, pl.ds(16, 128), :] = jnp.dot(val, flip, preferred_element_type=F32)
    for c in range(4):
        xpad[c, pl.ds(0, 16), :] = zeros
        xpad[c, pl.ds(16, 128), :] = jnp.dot(x_ref[c].astype(BF), flip, preferred_element_type=F32)
        dpad[c, pl.ds(0, 128), :] = d_ref[c]
        dpad[c, pl.ds(128, 8), :] = jnp.zeros((8, 128), F32)
    for r in range(16):
        lanes = pl.ds(r * 128, 128)
        for part in range(2):
            hbank[part, :, lanes] = hpad[part, pl.ds(r + 1, 128), :].astype(BF)
        for c in range(4):
            xbank[c, :, lanes] = xpad[c, pl.ds(r + 1, 128), :].astype(BF)
    gacc[...] = jnp.zeros_like(gacc)
    lacc[...] = jnp.zeros_like(lacc)
    late = col >= 127 - row
    for q in range(8):
        def build(r, _):
            for c in range(4):
                m = q * 16 + r
                now = jnp.broadcast_to(dpad[c, pl.ds(m, 1), :], (128, 128))
                nxt = jnp.broadcast_to(dpad[c, pl.ds(m + 1, 1), :], (128, 128))
                pick = jnp.where(late, now, nxt)
                w_ref[pl.ds(pl.multiple_of(r * 128, 128), 128), pl.ds(c * 128, 128)] = pltpu.roll(pick, 1, 1, stride=1, stride_axis=0).astype(BF)
            return 0
        lax.fori_loop(0, 16, build, 0)
        rows = 16 * (q + 1)
        out = pl.ds(128 - rows, rows)
        gacc[out, :] += jnp.dot(hbank[0, pl.ds(0, rows), :], w_ref[...], preferred_element_type=F32) + jnp.dot(hbank[1, pl.ds(0, rows), :], w_ref[...], preferred_element_type=F32)
        for c in range(4):
            lacc[out, :] += jnp.dot(xbank[c, pl.ds(0, rows), :], w_ref[:, pl.ds(c * 128, 128)], preferred_element_type=F32)
    for c in range(4):
        g_ref[c] = gacc[:, pl.ds(c * 128, 128)]
    put = (127 - lagcol_ref[...] == col).astype(F32)
    l_ref[...] = jnp.dot(put, lacc[...], precision=lax.Precision.HIGHEST, preferred_element_type=F32)

def conv(d, x, h, lag_block):
    v = pl.BlockSpec(memory_space=pltpu.VMEM)
    return pl.pallas_call(conv_kernel,
        out_shape=(jax.ShapeDtypeStruct((4, 128, 128), F32), jax.ShapeDtypeStruct((128, 128), F32)),
        in_specs=[v] * 5, out_specs=(v, v),
        scratch_shapes=[pltpu.VMEM((4, 136, 128), F32), pltpu.VMEM((4, 144, 128), F32), pltpu.VMEM((2, 144, 128), F32),
            pltpu.VMEM((2, 128, 2048), BF), pltpu.VMEM((4, 128, 2048), BF), pltpu.VMEM((2048, 512), BF),
            pltpu.VMEM((128, 512), F32), pltpu.VMEM((128, 128), F32)],
        compiler_params=pltpu.CompilerParams(vmem_limit_bytes=48 << 20),
    )(d, x, h, lag_block[:, None], lag_block[None, :])


def body(inputs_x, grad_out, filter_blocks, lag_block):
    both = jnp.stack([grad_out, inputs_x]).astype(F32)
    both = both.reshape(2, 128, 4, 128).transpose(3, 2, 0, 1)
    both = lax.all_to_all(both.reshape(512, 2, 128), ("ctx", "ch"), 0, 0, tiled=True)
    both = both.reshape(128, 4, 2, 128).transpose(2, 1, 0, 3)
    mine = lax.dynamic_slice_in_dim(filter_blocks[0], lax.axis_index("ch") * 128, 128, 1)
    rows = lax.all_to_all(mine.T, "ctx", 0, 0, tiled=True)
    g, l = conv(both[0], both[1], rows, lag_block)
    g = g[:, ::-1].transpose(1, 0, 2).reshape(512, 128)
    g = lax.all_to_all(g, ("ctx", "ch"), 0, 0, tiled=True)
    grad_inputs = g.reshape(128, 4, 128).transpose(2, 1, 0).reshape(128, 512).astype(BF)
    l = lax.all_to_all(l, "ctx", 0, 0, tiled=True)
    return grad_inputs, l.T[None]


def solution(mesh):
    in_specs = (P("ctx", "ch"), P("ctx", "ch"), P("ctx", None, None), P())
    out_specs = (P("ctx", "ch"), P("ctx", None, "ch"))
    return jax.shard_map(body, mesh=mesh, in_specs=in_specs, out_specs=out_specs, check_vma=False)
```

time: 261 us -> 167 us (0.64)
  waiting for transfers between devices: 147 us -> 87.9 us
  Pallas kernels: 0 us -> 24.5 us
  local copies, waits for them, and re-layouts: 31.1 us -> 7.44 us
  matrix products: 19.7 us -> 0 us
  other arithmetic: 17.9 us -> 0.18 us
  starting transfers between devices: 29.2 us -> 46.1 us
  between operations: 14.4 us -> 0.77 us
    all_to_all x2 -> x4, waiting for transfers between devices: 128 us -> 87.9 us  [the longest x1 35.4 us: body(): lax.all_to_all(both.reshape(512, 2, 128), ('ctx', 'ch'), 0, 0, tiled=True)]
    pallas_call x0 -> x1, Pallas kernels: none -> 24.5 us  [conv(): pl.pallas_call(conv_kernel, out_shape=(jax.ShapeDtypeStruct((4, 128, 128)...]
    dot_general x7 -> x0, matrix products: 19.7 us -> none  [exact_dot(): jnp.dot(left, right, precision=lax.Precision.HIGHEST, preferred_element_t...]
    reduce_scatter x1 -> x0, waiting for transfers between devices: 18.5 us -> none  [body(): lax.psum_scatter(exact_dot(inv_table, lag_rows), 'ch', scatter_dimension=...]
    all_to_all x2 -> x4, starting transfers between devices: 29.1 us -> 46.1 us  [the longest x1 24.3 us: body(): lax.all_to_all(both.reshape(512, 2, 128), ('ctx', 'ch'), 0, 0, tiled=True)]
    sub x4 -> x0, other arithmetic: 7.6 us -> none  [correlate(): first = [prod_00[part] - spread * prod_11[part] for part in range(2)]]
    another operation x5 -> x4, local copies, waits for them, and re-layouts: 7.37 us -> 1.31 us  [body(): both = jnp.stack([grad_out, inputs_x]).astype(F32)]
    unnamed x26 -> x8, local copies, waits for them, and re-layouts: 8.07 us -> 2.91 us
  transfers between devices with their start and end apart: 3 -> 4, of which waited for: 3 -> 4; matrix products, arithmetic and copies ran while one was open for 2% -> 2% of each run, Pallas kernels for 0% -> 0%
where the time goes in v1:
time: 167 us
  waiting for transfers between devices  87.9 us (53%)
  starting transfers between devices  46.1 us (28%)
  Pallas kernels  24.5 us (15%)
  local copies, waits for them, and re-layouts  7.44 us (4%)
    all_to_all x1, waiting for transfers between devices, body(): lax.all_to_all(both.reshape(512, 2, 128), ('ctx', 'ch'), 0, 0, tiled=True)  35.4 us
    pallas_call x1, Pallas kernels, conv(): pl.pallas_call(conv_kernel, out_shape=(jax.ShapeDtypeStruct((4, 128, 128)...  24.5 us
    all_to_all x1, waiting for transfers between devices, body(): g = lax.all_to_all(g, ('ctx', 'ch'), 0, 0, tiled=True)  24.4 us
    all_to_all x1, starting transfers between devices, body(): lax.all_to_all(both.reshape(512, 2, 128), ('ctx', 'ch'), 0, 0, tiled=True)  24.3 us
    all_to_all x1, waiting for transfers between devices, body(): l = lax.all_to_all(l, 'ctx', 0, 0, tiled=True)  14.1 us
    all_to_all x1, waiting for transfers between devices, body(): rows = lax.all_to_all(mine.T, 'ctx', 0, 0, tiled=True)  14.1 us
    all_to_all x1, starting transfers between devices, body(): g = lax.all_to_all(g, ('ctx', 'ch'), 0, 0, tiled=True)  9.78 us
    all_to_all x1, starting transfers between devices, body(): l = lax.all_to_all(l, 'ctx', 0, 0, tiled=True)  6.55 us
  transfers between devices with their start and end apart: 4, of which 4 were waited for; matrix products, arithmetic and copies ran while one was open for 2% of the time, Pallas kernels for 0%

profile of v1, /device:TPU:1, one launch (start us, length us, event | category | flops | bytes accessed | tf_op | source)
XLA Modules:
  0.0 166.9 jit_solution(9099723778954047794)
XLA Ops:
  0.6 0.0 copy-start
  0.6 1.0 stack.10
  1.6 0.0 copy-start.2
  1.6 0.1 copy.26
  1.8 0.7 copy-done.2
  2.6 0.1 copy.25
  2.7 0.2 maximum_convert_fusion
  2.9 1.2 copy.27
  4.1 24.3 %all-to-all-start = ((f32[512,2,128]{2,1,0:T(2,128)}), f32[512,2,128]{2,1,0:T(2,128)S(1)}, u32[]{:S(2)}, u32[]{:S(2)}) async-start(f32[512,2,128]{2,1,0:T(2,128)} %copy.27), calls=%async_computation | async-start | bytes 1048576 | tf_op jit(solution)/shard_map/all_to_all | solution.py:72
  28.4 0.0 copy-done
  28.5 0.7 copy.30
  29.2 35.4 %all-to-all-done = f32[512,2,128]{2,1,0:T(2,128)S(1)} async-done(((f32[512,2,128]{2,1,0:T(2,128)}), f32[512,2,128]{2,1,0:T(2,128)S(1)}, u32[]{:S(2)}, u32[]{:S(2)}) %all-to-all-start) | async-done | bytes 524320 | tf_op jit(solution)/shard_map/all_to_all | solution.py:72
  64.6 5.5 %all-to-all-start.1 = ((f32[128,1,128]{2,1,0:T(1,128)}), f32[128,1,128]{2,1,0:T(1,128)S(1)}, u32[]{:S(2)}, u32[]{:S(2)}) async-start(f32[128,1,128]{2,1,0:T(1,128)} %bitcast.8), calls=%async_computation.1 | async-start | bytes 131072 | tf_op jit(solution)/shard_map/all_to_all | solution.py:75
  70.0 0.0 copy-start.1
  70.0 0.6 copy-done.1
  70.7 0.1 copy.31.lagcol_ref
  70.8 0.1 copy.42
  71.0 14.1 %all-to-all-done.1 = f32[128,1,128]{2,1,0:T(1,128)S(1)} async-done(((f32[128,1,128]{2,1,0:T(1,128)}), f32[128,1,128]{2,1,0:T(1,128)S(1)}, u32[]{:S(2)}, u32[]{:S(2)}) %all-to-all-start.1) | async-done | bytes 65568 | tf_op jit(solution)/shard_map/all_to_all | solution.py:75
  85.0 24.5 %shard_map.59 = (f32[4,128,128]{2,1,0:T(8,128)S(1)}, f32[128,128]{1,0:T(8,128)}) custom-call(f32[4,128,128]{2,1,0:T(8,128)S(1)} %get-tuple-element.15.d_ref, f32[4,128,128]{2,1,0:T(8,128)S(1)} %get-tuple-element.14.x_ref, f32[128,128]{1,0:T(8,128)S(1)} %bitcast.36, s32[128,1]{1,0:T(8,128)S(1)} %copy.31.lagcol_ref, s32[1,128]{1,0:T(1,128)S(1)} %bitcast.38), custom_call_target="tpu_custom_call" | custom-call | tf_op jit(solution)/shard_map/pallas_call | solution.py:59
  109.5 6.5 %all-to-all-start.3 = ((f32[128,1,128]{2,1,0:T(1,128)}), f32[128,1,128]{2,1,0:T(1,128)S(1)}, u32[]{:S(2)}, u32[]{:S(2)}) async-start(f32[128,1,128]{2,1,0:T(1,128)} %bitcast.20), calls=%async_computation.3 | async-start | bytes 131072 | tf_op jit(solution)/shard_map/all_to_all | solution.py:80
  116.1 0.1 rev.3
  116.2 0.9 copy.32
  117.1 14.1 %all-to-all-done.3 = f32[128,1,128]{2,1,0:T(1,128)S(1)} async-done(((f32[128,1,128]{2,1,0:T(1,128)}), f32[128,1,128]{2,1,0:T(1,128)S(1)}, u32[]{:S(2)}, u32[]{:S(2)}) %all-to-all-start.3) | async-done | bytes 65568 | tf_op jit(solution)/shard_map/all_to_all | solution.py:80
  131.2 9.8 %all-to-all-start.2 = ((f32[512,1,128]{2,1,0:T(1,128)}), f32[512,1,128]{2,1,0:T(1,128)S(1)}, u32[]{:S(2)}, u32[]{:S(2)}) async-start(f32[512,1,128]{2,1,0:T(1,128)} %bitcast.14), calls=%async_computation.2 | async-start | bytes 524288 | tf_op jit(solution)/shard_map/all_to_all | solution.py:78
  141.0 0.7 copy.38
  141.7 24.4 %all-to-all-done.2 = f32[512,1,128]{2,1,0:T(1,128)S(1)} async-done(((f32[512,1,128]{2,1,0:T(1,128)}), f32[512,1,128]{2,1,0:T(1,128)S(1)}, u32[]{:S(2)}, u32[]{:S(2)}) %all-to-all-start.2) | async-done | bytes 262176 | tf_op jit(solution)/shard_map/all_to_all | solution.py:78
  166.1 0.8 copy.37
  (5 shorter events, 0.1 us)
Async XLA Ops:
  0.6 27.8 %copy-start = (f32[1,128,512]{2,1,0:T(8,128)S(1)}, f32[1,128,512]{2,1,0:T(8,128)}, u32[]{:S(2)}) copy-start(f32[1,128,512]{2,1,0:T(8,128)} %param.6) | copy-start | bytes 786436
  1.6 0.9 copy-start.2
  4.1 60.4 %all-to-all-start = ((f32[512,2,128]{2,1,0:T(2,128)}), f32[512,2,128]{2,1,0:T(2,128)S(1)}, u32[]{:S(2)}, u32[]{:S(2)}) async-start(f32[512,2,128]{2,1,0:T(2,128)} %copy.27), calls=%async_computation | async-start | bytes 1048576 | tf_op jit(solution)/shard_map/all_to_all | solution.py:72
  64.6 20.5 %all-to-all-start.1 = ((f32[128,1,128]{2,1,0:T(1,128)}), f32[128,1,128]{2,1,0:T(1,128)S(1)}, u32[]{:S(2)}, u32[]{:S(2)}) async-start(f32[128,1,128]{2,1,0:T(1,128)} %bitcast.8), calls=%async_computation.1 | async-start | bytes 131072 | tf_op jit(solution)/shard_map/all_to_all | solution.py:75
  70.0 0.7 copy-start.1
  109.5 21.6 %all-to-all-start.3 = ((f32[128,1,128]{2,1,0:T(1,128)}), f32[128,1,128]{2,1,0:T(1,128)S(1)}, u32[]{:S(2)}, u32[]{:S(2)}) async-start(f32[128,1,128]{2,1,0:T(1,128)} %bitcast.20), calls=%async_computation.3 | async-start | bytes 131072 | tf_op jit(solution)/shard_map/all_to_all | solution.py:80
  131.2 34.9 %all-to-all-start.2 = ((f32[512,1,128]{2,1,0:T(1,128)}), f32[512,1,128]{2,1,0:T(1,128)S(1)}, u32[]{:S(2)}, u32[]{:S(2)}) async-start(f32[512,1,128]{2,1,0:T(1,128)} %bitcast.14), calls=%async_computation.2 | async-start | bytes 524288 | tf_op jit(solution)/shard_map/all_to_all | solution.py:78

commit v2 on v1

v2 whole, which is shorter than its diff:
```python
import jax
import jax.numpy as jnp
from jax import lax
from jax.experimental import pallas as pl
from jax.experimental.pallas import tpu as pltpu
from jax.sharding import PartitionSpec as P

BF = jnp.bfloat16
F32 = jnp.float32
MESH = pl.DeviceIdType.MESH
N = 128
NZ = 16


def kernel(x_ref, d_ref, f_ref, lag_ref, gi_ref, gf_ref,
           own_d, own_x, y_dh, y_x, r_dh, r_x, gout, r_g, f_g, lout, r_l,
           dpad, xpad, hpad, hbank, xbank, w, lacc, send, recv, local):
    i = lax.axis_index("ctx")
    g = lax.axis_index("ch")
    px, pz, pc = lax.div(i, 2 * NZ), lax.rem(lax.div(i, 2), NZ), lax.rem(i, 2)

    def peer(k):
        k = N - 1 - k
        s = lax.div(k, 8)
        odd = lax.rem(s, 2)
        dz = odd * lax.div(s + 1, 2) + (1 - odd) * (NZ - lax.div(s, 2))
        z = lax.rem(pz + dz, NZ)
        x = lax.rem(px + lax.rem(lax.div(k, 2), 4), 4)
        return x * (2 * NZ) + z * 2 + lax.rem(pc + lax.rem(k, 2), 2)

    bar = pltpu.get_barrier_semaphore()

    def greet(k, _):
        pl.semaphore_signal(bar, inc=1, device_id=(peer(k), g), device_id_type=MESH)
        return 0

    lax.fori_loop(0, N - 1, greet, 0)
    for k in range(1, 4):
        pl.semaphore_signal(bar, inc=1, device_id=(i, lax.rem(g + k, 4)), device_id_type=MESH)

    for c in range(4):
        lanes = pl.ds(c * N, N)
        own_d[c] = d_ref[:, lanes].astype(F32).T
        own_x[c] = x_ref[:, lanes].astype(F32).T
    y_dh[4] = f_ref[:, pl.ds(pl.multiple_of(g * N, N), N)].T

    pl.semaphore_wait(bar, N + 2)

    def put(src, dst, n, device):
        pltpu.make_async_remote_copy(src_ref=src, dst_ref=dst, send_sem=send.at[n], recv_sem=recv.at[n],
                                     device_id=device, device_id_type=MESH).start()

    def keep(src, dst, n):
        copy = pltpu.make_async_copy(src, dst, local.at[n])
        copy.start()
        return copy

    def arrived(ref, n):
        pltpu.make_async_copy(ref, ref, recv.at[n]).wait()

    def sent(ref, n):
        pltpu.make_async_copy(ref, ref, send.at[n]).wait()

    def exchange_y(src, dst, n):
        for k in (2, 1, 3):
            to = lax.rem(g + k, 4)
            put(src.at[to], dst.at[g], n, (i, to))
        return keep(src.at[g], dst.at[g], n)

    def exchange_ctx(src, dst, n, row=lambda p: p):
        def go(k, _):
            p = peer(k)
            put(src.at[:, row(p), :], dst.at[:, i, :], n, (p, g))
            return 0

        lax.fori_loop(0, N - 1, go, 0)
        return keep(src.at[:, row(i), :], dst.at[:, i, :], n)

    most = pl.ds(0, N - 1)
    kept_d = exchange_y(own_d, y_dh, 0)
    kept_x = exchange_y(own_x, y_x, 1)
    kept_d.wait()
    arrived(own_d.at[pl.ds(0, 3)], 0)
    kept_dh = exchange_ctx(y_dh, r_dh, 2)
    kept_x.wait()
    arrived(own_x.at[pl.ds(0, 3)], 1)
    kept_rx = exchange_ctx(y_x, r_x, 3)

    kept_dh.wait()
    arrived(r_dh.at[:, most, :], 2)
    col = lax.broadcasted_iota(jnp.int32, (N, N), 1)
    row = lax.broadcasted_iota(jnp.int32, (N, N), 0)
    flip = (row + col == N - 1).astype(BF)
    lag = jnp.broadcast_to(lag_ref[...], (N, N))
    h = jnp.dot((lag == row).astype(F32), r_dh[4], precision=lax.Precision.HIGHEST, preferred_element_type=F32)
    hi = h.astype(BF)
    lo = (h - hi.astype(F32)).astype(BF)
    zeros = jnp.zeros((16, N), F32)
    for part, val in enumerate((hi, lo)):
        hpad[part, pl.ds(0, 16), :] = zeros
        hpad[part, pl.ds(16, N), :] = jnp.dot(val, flip, preferred_element_type=F32)
    for c in range(4):
        dpad[c, pl.ds(0, N), :] = r_dh[c]
        dpad[c, pl.ds(N, 8), :] = jnp.zeros((8, N), F32)
    for r in range(16):
        for part in range(2):
            hbank[part, :, pl.ds(r * N, N)] = hpad[part, pl.ds(r + 1, N), :].astype(BF)

    late = col >= N - 1 - row

    def build(m, _):
        for c in range(4):
            now = jnp.broadcast_to(dpad[c, pl.ds(m, 1), :], (N, N))
            nxt = jnp.broadcast_to(dpad[c, pl.ds(m + 1, 1), :], (N, N))
            pick = jnp.where(late, now, nxt)
            w[pl.ds(pl.multiple_of(m * N, N), N), pl.ds(c * N, N)] = pltpu.roll(pick, 1, 1, stride=1, stride_axis=0).astype(BF)
        return 0

    lax.fori_loop(0, N, build, 0, unroll=4)
    gout[...] = jnp.zeros_like(gout)
    for q in range(8):
        rows = 16 * (q + 1)
        part = jnp.dot(hbank[0, pl.ds(0, rows), :], w[pl.ds(q * 2048, 2048), :], preferred_element_type=F32)
        part += jnp.dot(hbank[1, pl.ds(0, rows), :], w[pl.ds(q * 2048, 2048), :], preferred_element_type=F32)
        for c in range(4):
            gout[c, pl.ds(N - rows, rows), :] += part[:, c * N:(c + 1) * N]
    kept_g = exchange_ctx(gout, r_g, 4, lambda p: N - 1 - p)

    kept_rx.wait()
    arrived(r_x.at[:, most, :], 3)
    for c in range(4):
        xpad[c, pl.ds(0, 16), :] = zeros
        xpad[c, pl.ds(16, N), :] = jnp.dot(r_x[c].astype(BF), flip, preferred_element_type=F32)
    for r in range(16):
        for c in range(4):
            xbank[c, :, pl.ds(r * N, N)] = xpad[c, pl.ds(r + 1, N), :].astype(BF)
    lacc[...] = jnp.zeros_like(lacc)
    for q in range(8):
        rows = 16 * (q + 1)
        part = jnp.zeros((rows, N), F32)
        for c in range(4):
            part += jnp.dot(xbank[c, pl.ds(0, rows), :], w[pl.ds(q * 2048, 2048), pl.ds(c * N, N)], preferred_element_type=F32)
        lacc[pl.ds(N - rows, rows), :] += part
    back = (N - 1 - lag == row).astype(F32).T
    lout[0] = jnp.dot(back, lacc[...], precision=lax.Precision.HIGHEST, preferred_element_type=F32)
    kept_l = exchange_ctx(lout, r_l, 5)

    kept_g.wait()
    arrived(r_g.at[:, most, :], 4)
    kept_f = exchange_y(r_g, f_g, 6)
    kept_l.wait()
    arrived(r_l.at[:, most, :], 5)
    gf_ref[...] = r_l[0].T
    kept_f.wait()
    arrived(r_g.at[pl.ds(0, 3)], 6)
    for c in range(4):
        gi_ref[:, pl.ds(c * N, N)] = f_g[c].T.astype(BF)

    sent(own_d.at[pl.ds(0, 3)], 0)
    sent(own_x.at[pl.ds(0, 3)], 1)
    sent(y_dh.at[:, most, :], 2)
    sent(y_x.at[:, most, :], 3)
    sent(gout.at[:, most, :], 4)
    sent(lout.at[:, most, :], 5)
    sent(r_g.at[pl.ds(0, 3)], 6)


def body(inputs_x, grad_out, filter_blocks, lag_block):
    v = pl.BlockSpec(memory_space=pltpu.VMEM)
    block = pltpu.VMEM((4, N, N), F32)
    gi, gf = pl.pallas_call(
        kernel,
        out_shape=(jax.ShapeDtypeStruct((N, 4 * N), BF), jax.ShapeDtypeStruct((N, N), F32)),
        in_specs=[v] * 4,
        out_specs=(v, v),
        scratch_shapes=[
            block, block, pltpu.VMEM((5, N, N), F32), block, pltpu.VMEM((5, N, N), F32), block, block, block, block,
            pltpu.VMEM((1, N, N), F32), pltpu.VMEM((1, N, N), F32),
            pltpu.VMEM((4, N + 8, N), F32), pltpu.VMEM((4, N + 16, N), F32), pltpu.VMEM((2, N + 16, N), F32),
            pltpu.VMEM((2, N, 16 * N), BF), pltpu.VMEM((4, N, 16 * N), BF), pltpu.VMEM((N * N, 4 * N), BF),
            pltpu.VMEM((N, N), F32),
            pltpu.SemaphoreType.DMA((7,)), pltpu.SemaphoreType.DMA((7,)), pltpu.SemaphoreType.DMA((7,)),
        ],
        compiler_params=pltpu.CompilerParams(collective_id=0, has_side_effects=True, vmem_limit_bytes=44 << 20),
    )(inputs_x, grad_out, filter_blocks[0], lag_block[None, :])
    return gi, gf[None]


def solution(mesh):
    in_specs = (P("ctx", "ch"), P("ctx", "ch"), P("ctx", None, None), P())
    out_specs = (P("ctx", "ch"), P("ctx", None, "ch"))
    return jax.shard_map(body, mesh=mesh, in_specs=in_specs, out_specs=out_specs, check_vma=False)
```

time: 167 us -> 82.6 us (0.49)
  waiting for transfers between devices: 87.9 us -> 0 us
  Pallas kernels: 24.5 us -> 77 us
  starting transfers between devices: 46.1 us -> 0 us
  local copies, waits for them, and re-layouts: 7.44 us -> 4.69 us
    all_to_all x4 -> x0, waiting for transfers between devices: 87.9 us -> none  [the longest x1 35.4 us: body(): lax.all_to_all(both.reshape(512, 2, 128), ('ctx', 'ch'), 0, 0, tiled=True)]
    pallas_call x1, Pallas kernels: 24.5 us -> 77 us  [body(): pl.pallas_call(kernel, out_shape=(jax.ShapeDtypeStruct((N, 4 * N), BF), j...]
    all_to_all x4 -> x0, starting transfers between devices: 46.1 us -> none  [the longest x1 24.3 us: body(): lax.all_to_all(both.reshape(512, 2, 128), ('ctx', 'ch'), 0, 0, tiled=True)]
    unnamed x8 -> x10, local copies, waits for them, and re-layouts: 2.91 us -> 4.69 us
  transfers between devices with their start and end apart: 4 -> 0, of which waited for: 4 -> 0; matrix products, arithmetic and copies ran while one was open for 2% -> 0% of each run, Pallas kernels for 0% -> 0%
where the time goes in v2:
time: 82.6 us; the launch traced here: 82.4 us
  Pallas kernels  77 us (93%)
  local copies, waits for them, and re-layouts  4.69 us (6%)
    pallas_call x1, Pallas kernels, body(): pl.pallas_call(kernel, out_shape=(jax.ShapeDtypeStruct((N, 4 * N), BF), j...  77 us
    unnamed x10, local copies, waits for them, and re-layouts  4.69 us

profile of v2, /device:TPU:1, one launch (start us, length us, event | category | flops | bytes accessed | tf_op | source)
XLA Modules:
  0.0 82.4 jit_solution(15725438210693516570)
XLA Ops:
  0.6 0.0 copy-start.3
  0.6 0.6 copy-done.3
  1.3 0.0 copy-start
  1.3 0.9 %copy-done = f32[1,128,512]{2,1,0:T(8,128)S(1)} copy-done((f32[1,128,512]{2,1,0:T(8,128)S(1)}, f32[1,128,512]{2,1,0:T(8,128)}, u32[]{:S(2)}) %copy-start) | copy-done | bytes 262168
  2.2 0.0 copy-start.1
  2.2 0.9 %copy-done.1 = bf16[128,512]{1,0:T(8,128)(2,1)S(1)} copy-done((bf16[128,512]{1,0:T(8,128)(2,1)S(1)}, bf16[128,512]{1,0:T(8,128)(2,1)}, u32[]{:S(2)}) %copy-start.1) | copy-done | bytes 131096
  3.1 0.0 copy-start.2
  3.1 0.9 %copy-done.2 = bf16[128,512]{1,0:T(8,128)(2,1)S(1)} copy-done((bf16[128,512]{1,0:T(8,128)(2,1)S(1)}, bf16[128,512]{1,0:T(8,128)(2,1)}, u32[]{:S(2)}) %copy-start.2) | copy-done | bytes 131096
  4.0 77.0 %shard_map.59 = (bf16[128,512]{1,0:T(8,128)(2,1)S(1)}, f32[128,128]{1,0:T(8,128)S(1)}) custom-call(bf16[128,512]{1,0:T(8,128)(2,1)S(1)} %copy-done.1, bf16[128,512]{1,0:T(8,128)(2,1)S(1)} %copy-done.2, f32[128,512]{1,0:T(8,128)S(1)} %bitcast.3, s32[1,128]{1,0:T(1,128)S(1)} %bitcast.5), custom_call_target="tpu_custom_call" | custom-call | tf_op jit(solution)/shard_map/pallas_call | solution.py:171
  81.1 0.7 copy.8
  81.7 0.6 copy.9
Async XLA Ops:
  0.6 0.7 copy-start.3
  1.3 0.9 %copy-start = (f32[1,128,512]{2,1,0:T(8,128)S(1)}, f32[1,128,512]{2,1,0:T(8,128)}, u32[]{:S(2)}) copy-start(f32[1,128,512]{2,1,0:T(8,128)} %param.6) | copy-start | bytes 786436
  2.2 0.9 %copy-start.1 = (bf16[128,512]{1,0:T(8,128)(2,1)S(1)}, bf16[128,512]{1,0:T(8,128)(2,1)}, u32[]{:S(2)}) copy-start(bf16[128,512]{1,0:T(8,128)(2,1)} %x_ref.1) | copy-start | bytes 393220
  3.1 0.9 %copy-start.2 = (bf16[128,512]{1,0:T(8,128)(2,1)S(1)}, bf16[128,512]{1,0:T(8,128)(2,1)}, u32[]{:S(2)}) copy-start(bf16[128,512]{1,0:T(8,128)(2,1)} %d_ref.1) | copy-start | bytes 393220

commit v3 on v1

v3 whole, which is shorter than its diff:
```python
import jax
import jax.numpy as jnp
from jax import lax
from jax.experimental import pallas as pl
from jax.experimental.pallas import tpu as pltpu
from jax.sharding import PartitionSpec as P

BF = jnp.bfloat16
F32 = jnp.float32
MESH = pl.DeviceIdType.MESH
N = 128
NZ = 16


def kernel(x_hbm, d_hbm, f_hbm, lag_hbm, gi_ref, gf_ref,
           x_in, d_in, f_in, lag_in, own_d, own_x, y_dh, y_x, r_dh, r_x, gout, r_g, f_g,
           dpad, xpad, hpad, hbank, xbank, w, lacc, send, recv, local):
    i = lax.axis_index("ctx")
    g = lax.axis_index("ch")
    px, pz, pc = lax.div(i, 2 * NZ), lax.rem(lax.div(i, 2), NZ), lax.rem(i, 2)
    around = [lax.rem(px + k, 4) * (2 * NZ) + lax.rem(pc + m, 2) for k in (0, 2, 1, 3) for m in (0, 1)]

    def each_peer(act):
        def at_distance(t, _):
            s = NZ - 1 - t
            odd = lax.rem(s, 2)
            dz = odd * lax.div(s + 1, 2) + (1 - odd) * (NZ - lax.div(s, 2))
            z = 2 * lax.rem(pz + dz, NZ)
            for a in around:
                act(a + z)
            return 0

        lax.fori_loop(0, NZ - 1, at_distance, 0)
        for a in around[1:]:
            act(a + 2 * pz)

    def keep(src, dst, n):
        copy = pltpu.make_async_copy(src, dst, local.at[n])
        copy.start()
        return copy

    def group(k):
        return lax.rem(g + k, 4)

    def lanes(k):
        return pl.ds(pl.multiple_of(group(k) * N, N), N)

    def greet(p):
        pl.semaphore_signal(bar, inc=1, device_id=(p, g), device_id_type=MESH)

    bar = pltpu.get_barrier_semaphore()
    for k in range(1, 4):
        pl.semaphore_signal(bar, inc=1, device_id=(i, group(k)), device_id_type=MESH)
    each_peer(greet)

    loads = [keep(d_hbm, d_in, 0), keep(f_hbm.at[0, :, lanes(0)], f_in, 1), keep(x_hbm, x_in, 2), keep(lag_hbm, lag_in, 3)]

    loads[0].wait()
    for k in range(1, 4):
        own_d[k - 1] = d_in[:, lanes(k)].astype(F32).T
    y_dh[1] = d_in[:, lanes(0)].astype(F32).T
    loads[1].wait()
    y_dh[0] = f_in[...].T
    loads[2].wait()
    for k in range(1, 4):
        own_x[k - 1] = x_in[:, lanes(k)].astype(F32).T
    y_x[0] = x_in[:, lanes(0)].astype(F32).T
    loads[3].wait()

    pl.semaphore_wait(bar, N + 2)

    def put(src, dst, n, device):
        pltpu.make_async_remote_copy(src_ref=src, dst_ref=dst, send_sem=send.at[n], recv_sem=recv.at[n],
                                     device_id=device, device_id_type=MESH).start()

    def arrived(ref, n):
        pltpu.make_async_copy(ref, ref, recv.at[n]).wait()

    def sent(ref, n):
        pltpu.make_async_copy(ref, ref, send.at[n]).wait()

    def exchange_ch(src, dst, n):
        for k in (2, 1, 3):
            put(src.at[k - 1], dst.at[3 - k], n, (i, group(k)))

    def exchange_ctx(src, dst, n, row=lambda p: p):
        each_peer(lambda p: put(src.at[:, row(p), :], dst.at[:, i, :], n, (p, g)))
        return keep(src.at[:, row(i), :], dst.at[:, i, :], n)

    most = pl.ds(0, N - 1)
    first, others = pl.ds(0, 2), pl.ds(2, 3)
    exchange_ch(own_d, y_dh.at[others], 0)
    exchange_ch(own_x, y_x.at[pl.ds(1, 3)], 1)
    kept_a = exchange_ctx(y_dh.at[first], r_dh.at[first], 4)
    arrived(own_d, 0)
    kept_b = exchange_ctx(y_dh.at[others], r_dh.at[others], 5)
    arrived(own_x, 1)
    kept_x = exchange_ctx(y_x, r_x, 6)

    col = lax.broadcasted_iota(jnp.int32, (N, N), 1)
    row = lax.broadcasted_iota(jnp.int32, (N, N), 0)
    flip = (row + col == N - 1).astype(BF)
    lag = jnp.broadcast_to(lag_in[...], (N, N))
    zeros = jnp.zeros((16, N), F32)
    late = col >= N - 1 - row

    def build(chans, unroll):
        for c in chans:
            dpad[c, pl.ds(0, N), :] = r_dh[c + 1]
            dpad[c, pl.ds(N, 8), :] = jnp.zeros((8, N), F32)

        def block(m, _):
            for c in chans:
                now = jnp.broadcast_to(dpad[c, pl.ds(m, 1), :], (N, N))
                nxt = jnp.broadcast_to(dpad[c, pl.ds(m + 1, 1), :], (N, N))
                pick = jnp.where(late, now, nxt)
                w[pl.ds(pl.multiple_of(m * N, N), N), pl.ds(c * N, N)] = pltpu.roll(pick, 1, 1, stride=1, stride_axis=0).astype(BF)
            return 0

        lax.fori_loop(0, N, block, 0, unroll=unroll)

    def grad_rows(c0, count, slot):
        for q in range(7, -1, -1):
            rows = 16 * (q + 1)
            part = jnp.dot(hbank[pl.ds(0, 2 * rows), :], w[pl.ds(q * 2048, 2048), pl.ds(c0 * N, count * N)], preferred_element_type=F32)
            part = part.reshape(q + 1, 2, 16, count * N)
            part = (part[:, 0] + part[:, 1]).reshape(rows, count * N)
            for c in range(count):
                if q == 7:
                    gout[slot + c] = part[:, c * N:(c + 1) * N]
                else:
                    gout[slot + c, pl.ds(N - rows, rows), :] += part[:, c * N:(c + 1) * N]

    kept_a.wait()
    arrived(r_dh.at[first, most, :], 4)
    h = jnp.dot((lag == row).astype(F32), r_dh[0], precision=lax.Precision.HIGHEST, preferred_element_type=F32)
    hi = h.astype(BF)
    lo = (h - hi.astype(F32)).astype(BF)
    for part, val in enumerate((hi, lo)):
        hpad[part, pl.ds(0, 16), :] = zeros
        hpad[part, pl.ds(16, N), :] = jnp.dot(val, flip, preferred_element_type=F32)
    for r in range(16):
        for part in range(2):
            val = hpad[part, pl.ds(r + 1, N), :].astype(BF)
            for t in range(8):
                hbank[pl.ds(32 * t + 16 * part, 16), pl.ds(r * N, N)] = val[16 * t:16 * t + 16]
    build((0,), 16)
    grad_rows(0, 1, 3)

    kept_b.wait()
    arrived(r_dh.at[others, most, :], 5)
    build((1, 2, 3), 4)
    grad_rows(1, 3, 0)
    early, last = pl.ds(0, 3), pl.ds(3, 2)
    kept_c = exchange_ctx(gout.at[early], r_g.at[early], 7, lambda p: N - 1 - p)

    kept_x.wait()
    arrived(r_x.at[:, most, :], 6)
    for c in range(4):
        xpad[c, pl.ds(0, 16), :] = zeros
        xpad[c, pl.ds(16, N), :] = jnp.dot(r_x[c].astype(BF), flip, preferred_element_type=F32)
    for r in range(16):
        for c in range(4):
            xbank[c, :, pl.ds(r * N, N)] = xpad[c, pl.ds(r + 1, N), :].astype(BF)
    for q in range(7, -1, -1):
        rows = 16 * (q + 1)
        part = jnp.zeros((rows, N), F32)
        for c in range(4):
            part += jnp.dot(xbank[c, pl.ds(0, rows), :], w[pl.ds(q * 2048, 2048), pl.ds(c * N, N)], preferred_element_type=F32)
        if q == 7:
            lacc[...] = part
        else:
            lacc[pl.ds(N - rows, rows), :] += part
    back = (N - 1 - lag == row).astype(BF)
    back = lax.dot_general(flip, back, (((1,), (1,)), ((), ())), preferred_element_type=F32)
    gout[4] = jnp.dot(back, lacc[...], precision=lax.Precision.HIGHEST, preferred_element_type=F32)
    kept_d = exchange_ctx(gout.at[last], r_g.at[last], 8, lambda p: N - 1 - p)

    kept_c.wait()
    arrived(r_g.at[early, most, :], 7)
    exchange_ch(r_g.at[early], f_g, 2)
    kept_d.wait()
    arrived(r_g.at[last, most, :], 8)
    gf_ref[...] = r_g[4].T
    gi_ref[:, lanes(0)] = r_g[3].T.astype(BF)
    arrived(f_g, 2)
    for k in range(1, 4):
        gi_ref[:, lanes(k)] = f_g[k - 1].T.astype(BF)

    sent(own_d, 0)
    sent(own_x, 1)
    sent(f_g, 2)
    sent(y_dh.at[first, most, :], 4)
    sent(y_dh.at[others, most, :], 5)
    sent(y_x.at[:, most, :], 6)
    sent(gout.at[early, most, :], 7)
    sent(gout.at[last, most, :], 8)


def body(inputs_x, grad_out, filter_blocks, lag_block):
    v = pl.BlockSpec(memory_space=pltpu.VMEM)

    def rows(n):
        return pltpu.VMEM((n, N, N), F32)

    gi, gf = pl.pallas_call(
        kernel,
        out_shape=(jax.ShapeDtypeStruct((N, 4 * N), BF), jax.ShapeDtypeStruct((N, N), F32)),
        in_specs=[pl.BlockSpec(memory_space=pltpu.HBM)] * 4,
        out_specs=(v, v),
        scratch_shapes=[
            pltpu.VMEM((N, 4 * N), BF), pltpu.VMEM((N, 4 * N), BF), pltpu.VMEM((N, N), F32), pltpu.VMEM((1, N), jnp.int32),
            rows(3), rows(3), rows(5), rows(4), rows(5), rows(4), rows(5), rows(5), rows(3),
            pltpu.VMEM((4, N + 8, N), F32), pltpu.VMEM((4, N + 16, N), F32), pltpu.VMEM((2, N + 16, N), F32),
            pltpu.VMEM((2 * N, 16 * N), BF), pltpu.VMEM((4, N, 16 * N), BF), pltpu.VMEM((N * N, 4 * N), BF),
            pltpu.VMEM((N, N), F32),
            pltpu.SemaphoreType.DMA((9,)), pltpu.SemaphoreType.DMA((9,)), pltpu.SemaphoreType.DMA((9,)),
        ],
        compiler_params=pltpu.CompilerParams(collective_id=0, has_side_effects=True, vmem_limit_bytes=56 << 20),
    )(inputs_x, grad_out, filter_blocks, lag_block[None, :])
    return gi, gf[None]


def solution(mesh):
    in_specs = (P("ctx", "ch"), P("ctx", "ch"), P("ctx", None, None), P())
    out_specs = (P("ctx", "ch"), P("ctx", None, "ch"))
    return jax.shard_map(body, mesh=mesh, in_specs=in_specs, out_specs=out_specs, check_vma=False)
```

time: 167 us -> 71.1 us (0.43)
  waiting for transfers between devices: 87.9 us -> 0 us
  starting transfers between devices: 46.1 us -> 0 us
  Pallas kernels: 24.5 us -> 68.1 us
  local copies, waits for them, and re-layouts: 7.44 us -> 2.23 us
    all_to_all x4 -> x0, waiting for transfers between devices: 87.9 us -> none  [the longest x1 35.4 us: body(): lax.all_to_all(both.reshape(512, 2, 128), ('ctx', 'ch'), 0, 0, tiled=True)]
    all_to_all x4 -> x0, starting transfers between devices: 46.1 us -> none  [the longest x1 24.3 us: body(): lax.all_to_all(both.reshape(512, 2, 128), ('ctx', 'ch'), 0, 0, tiled=True)]
    pallas_call x1, Pallas kernels: 24.5 us -> 68.1 us  [body(): pl.pallas_call(kernel, out_shape=(jax.ShapeDtypeStruct((N, 4 * N), BF), j...]
  transfers between devices with their start and end apart: 4 -> 0, of which waited for: 4 -> 0; matrix products, arithmetic and copies ran while one was open for 2% -> 0% of each run, Pallas kernels for 0% -> 0%
where the time goes in v3:
time: 71.1 us; the launch traced here: 71 us
  Pallas kernels  68.1 us (96%)
  local copies, waits for them, and re-layouts  2.23 us (3%)
    pallas_call x1, Pallas kernels, body(): pl.pallas_call(kernel, out_shape=(jax.ShapeDtypeStruct((N, 4 * N), BF), j...  68.1 us
    unnamed x4, local copies, waits for them, and re-layouts  2.23 us

profile of v3, /device:TPU:1, one launch (start us, length us, event | category | flops | bytes accessed | tf_op | source)
XLA Modules:
  0.0 71.0 jit_solution(1465699227925844839)
XLA Ops:
  0.6 68.1 %shard_map.59 = (bf16[128,512]{1,0:T(8,128)(2,1)}, f32[128,128]{1,0:T(8,128)}) custom-call(bf16[128,512]{1,0:T(8,128)(2,1)} %x_hbm.1, bf16[128,512]{1,0:T(8,128)(2,1)} %d_hbm.1, f32[1,128,512]{2,1,0:T(8,128)} %f_hbm.1, s32[1,128]{1,0:T(1,128)} %bitcast.3), custom_call_target="tpu_custom_call" | custom-call | tf_op jit(solution)/shard_map/pallas_call | solution.py:206
  68.7 0.0 copy-start
  68.7 1.6 %copy.8 = bf16[128,512]{1,0:T(8,128)(2,1)} copy(bf16[128,512]{1,0:T(8,128)(2,1)} %get-tuple-element.8) | data formatting | bytes 262144
  70.3 0.0 copy-done
  70.3 0.6 copy.9
Async XLA Ops:
  68.7 1.6 %copy-start = (f32[128,128]{1,0:T(8,128)S(1)}, f32[128,128]{1,0:T(8,128)}, u32[]{:S(2)}) copy-start(f32[128,128]{1,0:T(8,128)} %get-tuple-element.5) | copy-start | bytes 196612

commit v4 on v3

--- a/solution.py
+++ b/solution.py
@@ -93,9 +93,7 @@
     exchange_ch(own_x, y_x.at[pl.ds(1, 3)], 1)
     kept_a = exchange_ctx(y_dh.at[first], r_dh.at[first], 4)
     arrived(own_d, 0)
-    kept_b = exchange_ctx(y_dh.at[others], r_dh.at[others], 5)
-    arrived(own_x, 1)
-    kept_x = exchange_ctx(y_x, r_x, 6)
+    kept_b = [exchange_ctx(y_dh.at[pl.ds(c + 1, 1)], r_dh.at[pl.ds(c + 1, 1)], 8 + c) for c in (1, 2, 3)]
 
     col = lax.broadcasted_iota(jnp.int32, (N, N), 1)
     row = lax.broadcasted_iota(jnp.int32, (N, N), 0)
@@ -145,14 +143,18 @@
             for t in range(8):
                 hbank[pl.ds(32 * t + 16 * part, 16), pl.ds(r * N, N)] = val[16 * t:16 * t + 16]
     build((0,), 16)
-    grad_rows(0, 1, 3)
-
-    kept_b.wait()
-    arrived(r_dh.at[others, most, :], 5)
-    build((1, 2, 3), 4)
+
+    for c in (1, 2, 3):
+        kept_b[c - 1].wait()
+        arrived(r_dh.at[pl.ds(c + 1, 1), most, :], 8 + c)
+        if c == 1:
+            arrived(own_x, 1)
+            kept_x = exchange_ctx(y_x, r_x, 6)
+        build((c,), 16)
     grad_rows(1, 3, 0)
     early, last = pl.ds(0, 3), pl.ds(3, 2)
     kept_c = exchange_ctx(gout.at[early], r_g.at[early], 7, lambda p: N - 1 - p)
+    grad_rows(0, 1, 3)
 
     kept_x.wait()
     arrived(r_x.at[:, most, :], 6)
@@ -191,7 +193,8 @@
     sent(own_x, 1)
     sent(f_g, 2)
     sent(y_dh.at[first, most, :], 4)
-    sent(y_dh.at[others, most, :], 5)
+    for c in (1, 2, 3):
+        sent(y_dh.at[pl.ds(c + 1, 1), most, :], 8 + c)
     sent(y_x.at[:, most, :], 6)
     sent(gout.at[early, most, :], 7)
     sent(gout.at[last, most, :], 8)
@@ -214,9 +217,9 @@
             pltpu.VMEM((4, N + 8, N), F32), pltpu.VMEM((4, N + 16, N), F32), pltpu.VMEM((2, N + 16, N), F32),
             pltpu.VMEM((2 * N, 16 * N), BF), pltpu.VMEM((4, N, 16 * N), BF), pltpu.VMEM((N * N, 4 * N), BF),
             pltpu.VMEM((N, N), F32),
-            pltpu.SemaphoreType.DMA((9,)), pltpu.SemaphoreType.DMA((9,)), pltpu.SemaphoreType.DMA((9,)),
+            pltpu.SemaphoreType.DMA((12,)), pltpu.SemaphoreType.DMA((12,)), pltpu.SemaphoreType.DMA((12,)),
         ],
-        compiler_params=pltpu.CompilerParams(collective_id=0, has_side_effects=True, vmem_limit_bytes=56 << 20),
+        compiler_params=pltpu.CompilerParams(collective_id=0, has_side_effects=True, vmem_limit_bytes=int(53.65 * 2**20)),
     )(inputs_x, grad_out, filter_blocks, lag_block[None, :])
     return gi, gf[None]
 

time: 71.1 us -> 67.8 us (0.954)
  Pallas kernels: 68.1 us -> 65.1 us
    pallas_call x1, Pallas kernels: 68.1 us -> 65.1 us  [body(): pl.pallas_call(kernel, out_shape=(jax.ShapeDtypeStruct((N, 4 * N), BF), j...]
where the time goes in v4:
time: 67.8 us; the launch traced here: 67.6 us
  Pallas kernels  65.1 us (96%)
  local copies, waits for them, and re-layouts  1.94 us (3%)
    pallas_call x1, Pallas kernels, body(): pl.pallas_call(kernel, out_shape=(jax.ShapeDtypeStruct((N, 4 * N), BF), j...  65.1 us
    unnamed x4, local copies, waits for them, and re-layouts  1.94 us

profile of v4, /device:TPU:1, one launch (start us, length us, event | category | flops | bytes accessed | tf_op | source)
XLA Modules:
  0.0 67.6 jit_solution(10121251205755152255)
XLA Ops:
  0.6 0.0 copy-start
  0.6 0.6 copy-done
  1.3 65.1 %shard_map.59 = (bf16[128,512]{1,0:T(8,128)(2,1)S(1)}, f32[128,128]{1,0:T(8,128)S(1)}) custom-call(bf16[128,512]{1,0:T(8,128)(2,1)} %x_hbm.1, bf16[128,512]{1,0:T(8,128)(2,1)} %d_hbm.1, f32[1,128,512]{2,1,0:T(8,128)} %f_hbm.1, s32[1,128]{1,0:T(1,128)S(1)} %bitcast.3), custom_call_target="tpu_custom_call" | custom-call | tf_op jit(solution)/shard_map/pallas_call | solution.py:209
  66.4 0.7 copy.8
  67.0 0.6 copy.9
Async XLA Ops:
  0.6 0.7 copy-start

commit v5 on v4

--- a/solution.py
+++ b/solution.py
@@ -48,12 +48,11 @@
     def greet(p):
         pl.semaphore_signal(bar, inc=1, device_id=(p, g), device_id_type=MESH)
 
+    loads = [keep(d_hbm, d_in, 0), keep(f_hbm.at[0, :, lanes(0)], f_in, 1), keep(x_hbm, x_in, 2), keep(lag_hbm, lag_in, 3)]
     bar = pltpu.get_barrier_semaphore()
     for k in range(1, 4):
         pl.semaphore_signal(bar, inc=1, device_id=(i, group(k)), device_id_type=MESH)
     each_peer(greet)
-
-    loads = [keep(d_hbm, d_in, 0), keep(f_hbm.at[0, :, lanes(0)], f_in, 1), keep(x_hbm, x_in, 2), keep(lag_hbm, lag_in, 3)]
 
     loads[0].wait()
     for k in range(1, 4):
@@ -61,37 +60,37 @@
     y_dh[1] = d_in[:, lanes(0)].astype(F32).T
     loads[1].wait()
     y_dh[0] = f_in[...].T
+
+    pl.semaphore_wait(bar, N + 2)
+
+    def put(src, dst, n, device):
+        pltpu.make_async_remote_copy(src_ref=src, dst_ref=dst, send_sem=send.at[n], recv_sem=recv.at[n],
+                                     device_id=device, device_id_type=MESH).start()
+
+    def arrived(ref, n):
+        pltpu.make_async_copy(ref, ref, recv.at[n]).wait()
+
+    def sent(ref, n):
+        pltpu.make_async_copy(ref, ref, send.at[n]).wait()
+
+    def exchange_ch(src, dst, n):
+        for k in (2, 1, 3):
+            put(src.at[k - 1], dst.at[3 - k], n, (i, group(k)))
+
+    def exchange_ctx(src, dst, n, row=lambda p: p):
+        each_peer(lambda p: put(src.at[:, row(p), :], dst.at[:, i, :], n, (p, g)))
+        return keep(src.at[:, row(i), :], dst.at[:, i, :], n)
+
+    most = pl.ds(0, N - 1)
+    first, others = pl.ds(0, 2), pl.ds(2, 3)
+    exchange_ch(own_d, y_dh.at[others], 0)
+    kept_a = exchange_ctx(y_dh.at[first], r_dh.at[first], 4)
     loads[2].wait()
     for k in range(1, 4):
         own_x[k - 1] = x_in[:, lanes(k)].astype(F32).T
     y_x[0] = x_in[:, lanes(0)].astype(F32).T
     loads[3].wait()
-
-    pl.semaphore_wait(bar, N + 2)
-
-    def put(src, dst, n, device):
-        pltpu.make_async_remote_copy(src_ref=src, dst_ref=dst, send_sem=send.at[n], recv_sem=recv.at[n],
-                                     device_id=device, device_id_type=MESH).start()
-
-    def arrived(ref, n):
-        pltpu.make_async_copy(ref, ref, recv.at[n]).wait()
-
-    def sent(ref, n):
-        pltpu.make_async_copy(ref, ref, send.at[n]).wait()
-
-    def exchange_ch(src, dst, n):
-        for k in (2, 1, 3):
-            put(src.at[k - 1], dst.at[3 - k], n, (i, group(k)))
-
-    def exchange_ctx(src, dst, n, row=lambda p: p):
-        each_peer(lambda p: put(src.at[:, row(p), :], dst.at[:, i, :], n, (p, g)))
-        return keep(src.at[:, row(i), :], dst.at[:, i, :], n)
-
-    most = pl.ds(0, N - 1)
-    first, others = pl.ds(0, 2), pl.ds(2, 3)
-    exchange_ch(own_d, y_dh.at[others], 0)
     exchange_ch(own_x, y_x.at[pl.ds(1, 3)], 1)
-    kept_a = exchange_ctx(y_dh.at[first], r_dh.at[first], 4)
     arrived(own_d, 0)
     kept_b = [exchange_ctx(y_dh.at[pl.ds(c + 1, 1)], r_dh.at[pl.ds(c + 1, 1)], 8 + c) for c in (1, 2, 3)]
 

time: 67.8 us -> 67.5 us (level)
  no operation moved by 1% of the time
where the time goes in v5:
time: 67.5 us; the launch traced here: 67.3 us
  Pallas kernels  64.7 us (96%)
  local copies, waits for them, and re-layouts  1.94 us (3%)
    pallas_call x1, Pallas kernels, body(): pl.pallas_call(kernel, out_shape=(jax.ShapeDtypeStruct((N, 4 * N), BF), j...  64.7 us
    unnamed x4, local copies, waits for them, and re-layouts  1.94 us

profile of v5, /device:TPU:1, one launch (start us, length us, event | category | flops | bytes accessed | tf_op | source)
XLA Modules:
  0.0 67.3 jit_solution(5994478346221970820)
XLA Ops:
  0.6 0.0 copy-start
  0.6 0.6 copy-done
  1.3 64.7 %shard_map.59 = (bf16[128,512]{1,0:T(8,128)(2,1)S(1)}, f32[128,128]{1,0:T(8,128)S(1)}) custom-call(bf16[128,512]{1,0:T(8,128)(2,1)} %x_hbm.1, bf16[128,512]{1,0:T(8,128)(2,1)} %d_hbm.1, f32[1,128,512]{2,1,0:T(8,128)} %f_hbm.1, s32[1,128]{1,0:T(1,128)S(1)} %bitcast.3), custom_call_target="tpu_custom_call" | custom-call | tf_op jit(solution)/shard_map/pallas_call | solution.py:208
  66.0 0.7 copy.8
  66.7 0.6 copy.9
Async XLA Ops:
  0.6 0.7 copy-start
